TPU v7x, 512 devices: a whole 4x4x16 slice. The times are simulated.
512 devices in a mesh: ctx: 32 (over y, z_hi, core), fsdp: 16 (over z_lo, x).
Axes of the slice: x: 4, y: 4, z: 16 (z_hi: 4, z_lo: 4; z = z_hi * 4 + z_lo), core: 2. Of those that a mesh axis runs over, the one named last changes fastest.
Arguments:
- events: bfloat16 [8192, 4096], P('ctx'), may hold values from -6 to 6
- tile_mask: int32 [64, 2], P('ctx'), may hold values 0 or 1
- initial_state: float32 [16, 128, 128], P('fsdp'), may hold values from -96 to 96
- w_query: bfloat16 [4096, 2048], P('ctx', 'fsdp'), may hold values from -0.09375 to 0.09375
- w_key: bfloat16 [4096, 2048], P('ctx', 'fsdp'), may hold values from -0.09375 to 0.09375
- w_value: bfloat16 [4096, 2048], P('ctx', 'fsdp'), may hold values from -0.09375 to 0.09375
- cotangent: bfloat16 [8192, 2048], P('ctx', 'fsdp'), may hold values from -6 to 6
Outputs:
- attended: bfloat16 [8192, 2048], P('ctx', 'fsdp')
- events_grad: bfloat16 [8192, 4096], P('ctx')
- query_grad: bfloat16 [4096, 2048], P('ctx', 'fsdp')
- key_grad: bfloat16 [4096, 2048], P('ctx', 'fsdp')
- value_grad: bfloat16 [4096, 2048], P('ctx', 'fsdp')
Inputs may be any that keep to these rules, and one draw needn't show every extreme that they name: `tile_mask`: only entries whose column is not above the row's tile place within its block of 256 events are read.
All inputs are finite; a program needn't handle non-finite values.
Results may differ from a plain program's by a relative error of at most 0.03.
Values may be sent and summed in bfloat16 or wider, within the bound.
No kernel may reach another device: no remote copies, remote signals or barrier semaphores. Data moves between devices by JAX's collectives and lax.ppermute only.
A program may use at most 64 MiB of HBM per device.

v0:
```python
import jax
import jax.numpy as jnp
from jax import lax
from jax.sharding import PartitionSpec as P

HDIM = 128
TILE = 128
epsilon = 1e-06


def prefix(array, axis, combine, identity, reverse):
    count, index = (lax.axis_size(axis), lax.axis_index(axis))
    everything = lax.all_gather(array.astype(jnp.bfloat16), axis)
    start = jnp.broadcast_to(jnp.asarray(identity, array.dtype), array.shape)

    def turn(k, before):
        at = count - 1 - k if reverse else k
        reached = at > index if reverse else at < index
        new = combine(before, everything[at].astype(array.dtype))
        return jnp.where(reached, new, before)

    return lax.fori_loop(0, count, turn, start)


def allowed_pairs(mask_block, tile):
    count = mask_block.shape[0]
    size = count * tile
    row_index = lax.broadcasted_iota(jnp.int32, (size, size), 0)
    col_index = lax.broadcasted_iota(jnp.int32, (size, size), 1)
    tiled = jnp.repeat(jnp.repeat(mask_block, tile, axis=0), tile, axis=1)
    return jnp.where((col_index <= row_index) & (tiled > 0), 1.0, 0.0).astype(jnp.float32)


def add_states(earlier, later):
    return earlier + later


def block_prefix(local_term, reverse):
    return prefix(local_term, "ctx", add_states, jnp.zeros_like(local_term), reverse)


def on_device(events, tile_mask, initial_state, w_query, w_key, w_value, cotangent):
    event_count, head_width = cotangent.shape
    head_count = head_width // HDIM
    stacked = jnp.stack((w_query, w_key, w_value))
    allowed = allowed_pairs(tile_mask, TILE)
    panels = lax.all_gather(stacked, "ctx", axis=1, tiled=True)
    projected = jnp.einsum("td,kdw->ktw", events, panels, preferred_element_type=jnp.float32)
    projected = projected.astype(jnp.bfloat16).reshape(3, event_count, head_count, HDIM)
    queries, key_rows, value_rows = (projected[0], projected[1], projected[2])
    local_state = jnp.einsum(
        "thd,the->hde", key_rows, value_rows, preferred_element_type=jnp.float32
    )
    carried_bf = (block_prefix(local_state, False) + initial_state).astype(jnp.bfloat16)
    scores = (
        jnp.einsum("thd,shd->hts", queries, key_rows, preferred_element_type=jnp.float32)
        * allowed[None]
    )
    mixing = scores.astype(jnp.bfloat16)
    mixture = jnp.einsum("hts,shd->thd", mixing, value_rows, preferred_element_type=jnp.float32)
    mixture = mixture + jnp.einsum(
        "thd,hde->the", queries, carried_bf, preferred_element_type=jnp.float32
    )
    inverse_rms = lax.rsqrt(jnp.mean(mixture * mixture, axis=-1, keepdims=True) + epsilon)
    attended = (mixture * inverse_rms).astype(jnp.bfloat16).reshape(event_count, head_width)
    upstream = cotangent.reshape(event_count, head_count, HDIM).astype(jnp.float32)
    mixture_grad = (
        inverse_rms * upstream
        - mixture * inverse_rms**3 * jnp.mean(upstream * mixture, axis=-1, keepdims=True)
    ).astype(jnp.bfloat16)
    score_grad = (
        jnp.einsum("the,she->hts", mixture_grad, value_rows, preferred_element_type=jnp.float32)
        * allowed[None]
    ).astype(jnp.bfloat16)
    local_grad = jnp.einsum(
        "thd,the->hde", queries, mixture_grad, preferred_element_type=jnp.float32
    )
    later_bf = block_prefix(local_grad, True).astype(jnp.bfloat16)
    query_part = jnp.einsum(
        "hts,shd->thd", score_grad, key_rows, preferred_element_type=jnp.float32
    )
    query_part = query_part + jnp.einsum(
        "the,hde->thd", mixture_grad, carried_bf, preferred_element_type=jnp.float32
    )
    key_part = jnp.einsum("hts,thd->shd", score_grad, queries, preferred_element_type=jnp.float32)
    key_part = key_part + jnp.einsum(
        "she,hde->shd", value_rows, later_bf, preferred_element_type=jnp.float32
    )
    value_part = jnp.einsum(
        "hts,the->she", mixing, mixture_grad, preferred_element_type=jnp.float32
    )
    value_part = value_part + jnp.einsum(
        "shd,hde->she", key_rows, later_bf, preferred_element_type=jnp.float32
    )
    grads = (
        jnp.stack((query_part, key_part, value_part))
        .astype(jnp.bfloat16)
        .reshape(3, event_count, head_width)
    )
    partial_grad = jnp.einsum("ktw,kdw->td", grads, panels, preferred_element_type=jnp.float32)
    events_grad = lax.psum(partial_grad.astype(jnp.bfloat16), "fsdp")
    summed = lax.psum_scatter(
        jnp.einsum("td,ktw->dkw", events, grads, preferred_element_type=jnp.float32).astype(
            jnp.bfloat16
        ),
        "ctx",
        scatter_dimension=0,
        tiled=True,
    )
    return (attended, events_grad, summed[:, 0], summed[:, 1], summed[:, 2])


def solution(mesh):
    placed = (
        P("ctx", None),
        P("ctx", None),
        P("fsdp", None, None),
        P("ctx", "fsdp"),
        P("ctx", "fsdp"),
        P("ctx", "fsdp"),
        P("ctx", "fsdp"),
    )
    return jax.shard_map(
        on_device,
        mesh=mesh,
        in_specs=placed,
        out_specs=(
            P("ctx", "fsdp"),
            P("ctx", None),
            P("ctx", "fsdp"),
            P("ctx", "fsdp"),
            P("ctx", "fsdp"),
        ),
        check_vma=False,
    )
```

profile of v0, /device:TPU:8, one launch (start us, length us, event | category | flops | bytes accessed | tf_op | source)
XLA Modules:
  0.0 613.5 jit_solution(2426722656759367331)
XLA Ops:
  7.2 1.0 copy.38
  8.2 0.9 copy.39
  9.1 0.9 copy.40
  10.8 97.0 %all-gather.6.cloned.1.call-done = bf16[3,4096,128]{1,2,0:T(8,128)(2,1)} async-done(((bf16[3,128,128]{1,2,0:T(8,128)(2,1)}), bf16[3,4096,128]{1,2,0:T(8,128)(2,1)}) %all-gather.6.cloned.1.call-update) | async-done | bytes 3145744 | tf_op jit(solution)/shard_map/all_gather | solution.py:47
  107.8 2.9 fusion.9
  112.3 63.8 %all-gather.8.cloned.1.call-done = bf16[4096,128]{1,0:T(8,128)(2,1)} async-done(((bf16[128,128]{1,0:T(8,128)(2,1)}), bf16[4096,128]{1,0:T(8,128)(2,1)}) %all-gather.8.cloned.1.call-update) | async-done | bytes 1048592 | tf_op jit(solution)/shard_map/all_gather | solution.py:13
  176.0 25.8 %while.30 = (s32[]{:T(128)}, f32[1,128,128]{2,1,0:T(8,128)S(1)}, s32[]{:T(128)}, bf16[32,1,128,128]{3,2,1,0:T(8,128)(2,1)}, s32[]{:T(128)}, /*index=5*/s32[]{:T(128)}) while((s32[]{:T(128)}, f32[1,128,128]{2,1,0:T(8,128)S(1)}, s32[]{:T(128)}, bf16[32,1,128,128]{3,2,1,0:T(8,128)(2,1)}, s32[]{:T(128)}, /*index=5*/s32[]{:T(128)}) %tuple.105), condition=%wide.region_1.2_spmd.clone, body=%wide.region_0.1_spmd.clone.sunk | while | flops 65540 | bytes 163941 | solution.py:22
  176.8 0.8 add_select_fusion.4
  177.7 0.8 add_select_fusion.4
  178.5 0.8 add_select_fusion.4
  179.3 0.8 add_select_fusion.4
  180.1 0.8 add_select_fusion.4
  180.9 0.8 add_select_fusion.4
  181.7 0.8 add_select_fusion.4
  182.5 0.8 add_select_fusion.4
  183.3 0.8 add_select_fusion.4
  184.1 0.8 add_select_fusion.4
  184.9 0.8 add_select_fusion.4
  185.7 0.8 add_select_fusion.4
  186.5 0.8 add_select_fusion.4
  187.3 0.8 add_select_fusion.4
  188.1 0.8 add_select_fusion.4
  188.9 0.8 add_select_fusion.4
  189.7 0.8 add_select_fusion.4
  190.6 0.8 add_select_fusion.4
  191.4 0.8 add_select_fusion.4
  192.2 0.8 add_select_fusion.4
  193.0 0.8 add_select_fusion.4
  193.8 0.8 add_select_fusion.4
  194.6 0.8 add_select_fusion.4
  196.2 0.8 add_select_fusion.4
  200.2 0.8 add_select_fusion.4
  203.8 65.0 %all-gather.10.cloned.1.call-done = bf16[4096,128]{1,0:T(8,128)(2,1)} async-done(((bf16[128,128]{1,0:T(8,128)(2,1)}), bf16[4096,128]{1,0:T(8,128)(2,1)}) %all-gather.10.cloned.1.call-update) | async-done | bytes 1048592 | tf_op jit(solution)/shard_map/all_gather | solution.py:13
  268.8 25.9 %while.31 = (s32[]{:T(128)}, f32[1,128,128]{2,1,0:T(8,128)S(1)}, s32[]{:T(128)}, bf16[32,1,128,128]{3,2,1,0:T(8,128)(2,1)}, s32[]{:T(128)}, /*index=5*/s32[]{:T(128)}, s32[]{:T(128)}, s32[]{:T(128)}) while((s32[]{:T(128)}, f32[1,128,128]{2,1,0:T(8,128)S(1)}, s32[]{:T(128)}, bf16[32,1,128,128]{3,2,1,0:T(8,128)(2,1)}, s32[]{:T(128)}, ...), condition=%wide.region_5.6_spmd.clone, body=%wide.region_4.5_spmd.clone.sunk | while | flops 65544 | bytes 164003 | solution.py:22
  269.6 0.8 add_select_fusion.5
  273.6 0.8 add_select_fusion.5
  276.1 0.8 add_select_fusion.5
  282.5 0.8 add_select_fusion.5
  285.0 0.8 add_select_fusion.5
  289.0 0.8 add_select_fusion.5
  291.5 0.8 add_select_fusion.5
  295.4 2.7 convolution_convert_fusion
  298.1 4.7 copy.56
  302.8 4.5 fusion
  308.1 118.9 %reduce-scatter.4.cloned.1.call-done = bf16[128,384]{1,0:T(8,128)(2,1)} async-done(((bf16[4096,384]{1,0:T(8,128)(2,1)}), bf16[128,384]{1,0:T(8,128)(2,1)}) %reduce-scatter.4.cloned.1.call-update) | async-done | bytes 98320
  427.0 1.0 copy.57
  430.2 173.7 %all-reduce.2.cloned.1.call-done = bf16[256,4096]{1,0:T(8,128)(2,1)} async-done(((bf16[256,4096]{1,0:T(8,128)(2,1)}), bf16[256,4096]{1,0:T(8,128)(2,1)}) %all-reduce.2.cloned.1.call-update) | async-done | bytes 2097168 | tf_op jit(solution)/shard_map/psum | solution.py:101
  603.8 3.1 copy.76
  (80 shorter events, 32.9 us)
Async XLA Ops:
  7.2 100.6 %copy-start = (bf16[256,4096]{1,0:T(8,128)(2,1)S(1)}, bf16[256,4096]{1,0:T(8,128)(2,1)}, u32[]{:S(2)}) copy-start(bf16[256,4096]{1,0:T(8,128)(2,1)} %param.11) | copy-start | bytes 6291460
  7.2 100.6 %all-gather.6.cloned.1.call-start = ((), (), s32[]{:S(2)}) async-start(), calls=%async_computation.1 | async-start | bytes 3244032 | tf_op jit(solution)/shard_map/all_gather | solution.py:47
  10.7 100.9 %copy-start.3 = (s32[2,2]{1,0:T(2,128)S(1)}, s32[2,2]{1,0:T(2,128)}, u32[]{:S(2)}) copy-start(s32[2,2]{1,0:T(2,128)} %param.12) | copy-start | bytes 52
  10.7 101.2 %copy-start.1 = (bf16[256,128]{1,0:T(8,128)(2,1)S(1)}, bf16[256,128]{1,0:T(8,128)(2,1)}, u32[]{:S(2)}) copy-start(bf16[256,128]{1,0:T(8,128)(2,1)} %param.17) | copy-start | bytes 196612
  10.7 191.1 %copy-start.2 = (f32[1,128,128]{2,1,0:T(8,128)S(1)}, f32[1,128,128]{2,1,0:T(8,128)}, u32[]{:S(2)}) copy-start(f32[1,128,128]{2,1,0:T(8,128)} %param.13) | copy-start | bytes 196612
  10.7 165.3 %all-gather.8.cloned.1.call-start = ((), (), s32[]{:S(2)}) async-start(), calls=%async_computation.3 | async-start | bytes 1081344 | tf_op jit(solution)/shard_map/all_gather | solution.py:13
  111.5 157.3 %all-gather.10.cloned.1.call-start = ((), (), s32[]{:S(2)}) async-start(), calls=%async_computation.4 | async-start | bytes 1081344 | tf_op jit(solution)/shard_map/all_gather | solution.py:13
  203.2 223.8 %reduce-scatter.4.cloned.1.call-start = ((), (), s32[]{:S(2)}) async-start(), calls=%async_computation.5 | async-start | bytes 3244032
  302.8 301.1 %all-reduce.2.cloned.1.call-start = ((), (), s32[]{:S(2)}) async-start(), calls=%async_computation.2 | async-start | bytes 4194304 | tf_op jit(solution)/shard_map/psum | solution.py:101
Sparse Core Ops, SparseCore 0:
  11.6 96.0 all-gather.5
  111.6 64.4 all-gather.7
  203.3 65.4 all-gather.9
  302.9 124.0 reduce-scatter.3
  430.6 173.1 all-reduce.1
where the time goes:
time: 618 us; the launch traced here: 613 us
  waiting for transfers between devices  518 us (84%)
  other arithmetic  50.9 us (8%)
  local copies, waits for them, and re-layouts  14.9 us (2%)
  between operations  14 us (2%)
  matrix products  13.5 us (2%)
    psum x1, waiting for transfers between devices, on_device(): events_grad = lax.psum(partial_grad.astype(jnp.bfloat16), 'fsdp')  174 us
    all_gather x2, waiting for transfers between devices, prefix(): everything = lax.all_gather(array.astype(jnp.bfloat16), axis)  129 us
    unnamed x6, waiting for transfers between devices  119 us
    all_gather x1, waiting for transfers between devices, on_device(): panels = lax.all_gather(stacked, 'ctx', axis=1, tiled=True)  97 us
    select_n x64, other arithmetic, turn(): return jnp.where(reached, new, before)  50.1 us
    unnamed x21, local copies, waits for them, and re-layouts  14.7 us
  transfers between devices with their start and end apart: 5, of which 5 were waited for; matrix products, arithmetic and copies ran while one was open for 2% of the time, Pallas kernels for 0%

commit v1 on v0

--- a/solution.py
+++ b/solution.py
@@ -44,7 +44,9 @@
     head_count = head_width // HDIM
     stacked = jnp.stack((w_query, w_key, w_value))
     allowed = allowed_pairs(tile_mask, TILE)
-    panels = lax.all_gather(stacked, "ctx", axis=1, tiled=True)
+    panels = jnp.concatenate(
+        lax.all_to_all(jnp.stack([stacked] * lax.axis_size("ctx")), "ctx", 0, 0), axis=1
+    )
     projected = jnp.einsum("td,kdw->ktw", events, panels, preferred_element_type=jnp.float32)
     projected = projected.astype(jnp.bfloat16).reshape(3, event_count, head_count, HDIM)
     queries, key_rows, value_rows = (projected[0], projected[1], projected[2])

time: 618 us -> 680 us (1.10)
  blocking collectives: 0 us -> 159 us
  waiting for transfers between devices: 518 us -> 424 us
    all_to_all x0 -> x1, blocking collectives: none -> 159 us  [on_device(): lax.all_to_all(jnp.stack([stacked] * lax.axis_size('ctx')), 'ctx', 0, 0)]
    all_gather x1 -> x0, waiting for transfers between devices: 97 us -> none  [on_device(): panels = lax.all_gather(stacked, 'ctx', axis=1, tiled=True)]
    unnamed x21 -> x20, local copies, waits for them, and re-layouts: 14.7 us -> 12.5 us
    unnamed x6 -> x5, waiting for transfers between devices: 119 us -> 119 us
  transfers between devices with their start and end apart: 5 -> 4, of which waited for: 5 -> 4; matrix products, arithmetic and copies ran while one was open for 2% -> 1% of each run, Pallas kernels for 0% -> 0%
where the time goes in v1:
time: 680 us; the launch traced here: 675 us
  waiting for transfers between devices  424 us (62%)
  blocking collectives  159 us (23%)
  other arithmetic  51.2 us (8%)
  between operations  14 us (2%)
  local copies, waits for them, and re-layouts  13.7 us (2%)
  matrix products  11.6 us (2%)
    psum x1, waiting for transfers between devices, on_device(): events_grad = lax.psum(partial_grad.astype(jnp.bfloat16), 'fsdp')  174 us
    all_to_all x1, blocking collectives, on_device(): lax.all_to_all(jnp.stack([stacked] * lax.axis_size('ctx')), 'ctx', 0, 0)  159 us
    all_gather x2, waiting for transfers between devices, prefix(): everything = lax.all_gather(array.astype(jnp.bfloat16), axis)  131 us
    unnamed x5, waiting for transfers between devices  119 us
    select_n x64, other arithmetic, turn(): return jnp.where(reached, new, before)  50.1 us
  transfers between devices with their start and end apart: 4, of which 4 were waited for; matrix products, arithmetic and copies ran while one was open for 1% of the time, Pallas kernels for 0%

profile of v1, /device:TPU:8, one launch (start us, length us, event | category | flops | bytes accessed | tf_op | source)
XLA Modules:
  0.0 675.1 jit_solution(5536399203788660780)
XLA Ops:
  7.2 0.9 pad_maximum_fusion.1
  9.1 158.9 %all_to_all.5 = bf16[32,3,128,128]{2,3,1,0:T(8,128)(2,1)S(1)} all-to-all(bf16[32,3,128,128]{2,3,1,0:T(8,128)(2,1)S(1)} %stack.22), channel_id=1, replica_groups=mesh['ctx'=32,'fsdp'=16] {'ctx'}, dimensions={0} | all-to-all | bytes 6291456 | tf_op jit(solution)/shard_map/all_to_all | solution.py:48
  168.0 1.0 fusion.15
  171.2 66.4 %all-gather.5.cloned.1.call-done = bf16[4096,128]{1,0:T(8,128)(2,1)} async-done(((bf16[128,128]{1,0:T(8,128)(2,1)}), bf16[4096,128]{1,0:T(8,128)(2,1)}) %all-gather.5.cloned.1.call-update) | async-done | bytes 1048592 | tf_op jit(solution)/shard_map/all_gather | solution.py:13
  237.6 25.8 %while.30 = (s32[]{:T(128)}, f32[1,128,128]{2,1,0:T(8,128)S(1)}, s32[]{:T(128)}, bf16[32,1,128,128]{3,2,1,0:T(8,128)(2,1)}, s32[]{:T(128)}, /*index=5*/s32[]{:T(128)}) while((s32[]{:T(128)}, f32[1,128,128]{2,1,0:T(8,128)S(1)}, s32[]{:T(128)}, bf16[32,1,128,128]{3,2,1,0:T(8,128)(2,1)}, s32[]{:T(128)}, /*index=5*/s32[]{:T(128)}) %tuple.103), condition=%wide.region_1.2_spmd.clone, body=%wide.region_0.1_spmd.clone.sunk | while | flops 65540 | bytes 163941 | solution.py:22
  238.4 0.8 add_select_fusion.4
  239.2 0.8 add_select_fusion.4
  240.0 0.8 add_select_fusion.4
  240.8 0.8 add_select_fusion.4
  241.6 0.8 add_select_fusion.4
  242.4 0.8 add_select_fusion.4
  243.2 0.8 add_select_fusion.4
  244.0 0.8 add_select_fusion.4
  244.8 0.8 add_select_fusion.4
  245.6 0.8 add_select_fusion.4
  246.4 0.8 add_select_fusion.4
  247.2 0.8 add_select_fusion.4
  248.1 0.8 add_select_fusion.4
  248.9 0.8 add_select_fusion.4
  249.7 0.8 add_select_fusion.4
  250.5 0.8 add_select_fusion.4
  251.3 0.8 add_select_fusion.4
  252.1 0.8 add_select_fusion.4
  252.9 0.8 add_select_fusion.4
  253.7 0.8 add_select_fusion.4
  254.5 0.8 add_select_fusion.4
  255.3 0.8 add_select_fusion.4
  256.1 0.8 add_select_fusion.4
  256.9 0.8 add_select_fusion.4
  257.7 0.8 add_select_fusion.4
  258.5 0.8 add_select_fusion.4
  259.3 0.8 add_select_fusion.4
  261.0 0.8 add_select_fusion.4
  265.3 65.0 %all-gather.7.cloned.1.call-done = bf16[4096,128]{1,0:T(8,128)(2,1)} async-done(((bf16[128,128]{1,0:T(8,128)(2,1)}), bf16[4096,128]{1,0:T(8,128)(2,1)}) %all-gather.7.cloned.1.call-update) | async-done | bytes 1048592 | tf_op jit(solution)/shard_map/all_gather | solution.py:13
  330.3 25.9 %while.31 = (s32[]{:T(128)}, f32[1,128,128]{2,1,0:T(8,128)S(1)}, s32[]{:T(128)}, bf16[32,1,128,128]{3,2,1,0:T(8,128)(2,1)}, s32[]{:T(128)}, /*index=5*/s32[]{:T(128)}, s32[]{:T(128)}, s32[]{:T(128)}) while((s32[]{:T(128)}, f32[1,128,128]{2,1,0:T(8,128)S(1)}, s32[]{:T(128)}, bf16[32,1,128,128]{3,2,1,0:T(8,128)(2,1)}, s32[]{:T(128)}, ...), condition=%wide.region_5.6_spmd.clone, body=%wide.region_4.5_spmd.clone.sunk | while | flops 65544 | bytes 164003 | solution.py:22
  334.4 0.8 add_select_fusion.5
  336.8 0.8 add_select_fusion.5
  343.3 0.8 add_select_fusion.5
  345.7 0.8 add_select_fusion.5
  349.8 0.8 add_select_fusion.5
  352.2 0.8 add_select_fusion.5
  356.9 2.7 convolution_convert_fusion
  359.6 4.7 copy.51
  364.4 4.5 fusion
  369.6 118.9 %reduce-scatter.4.cloned.1.call-done = bf16[128,384]{1,0:T(8,128)(2,1)} async-done(((bf16[4096,384]{1,0:T(8,128)(2,1)}), bf16[128,384]{1,0:T(8,128)(2,1)}) %reduce-scatter.4.cloned.1.call-update) | async-done | bytes 98320
  488.5 1.0 copy.52
  491.7 173.8 %all-reduce.2.cloned.1.call-done = bf16[256,4096]{1,0:T(8,128)(2,1)} async-done(((bf16[256,4096]{1,0:T(8,128)(2,1)}), bf16[256,4096]{1,0:T(8,128)(2,1)}) %all-reduce.2.cloned.1.call-update) | async-done | bytes 2097168 | tf_op jit(solution)/shard_map/psum | solution.py:103
  665.5 3.1 copy.84
  (79 shorter events, 32.1 us)
Async XLA Ops:
  7.2 160.8 %copy-start = (bf16[256,4096]{1,0:T(8,128)(2,1)S(1)}, bf16[256,4096]{1,0:T(8,128)(2,1)}, u32[]{:S(2)}) copy-start(bf16[256,4096]{1,0:T(8,128)(2,1)} %param.11) | copy-start | bytes 6291460
  7.2 230.4 %all-gather.5.cloned.1.call-start = ((), (), s32[]{:S(2)}) async-start(), calls=%async_computation.3 | async-start | bytes 1081344 | tf_op jit(solution)/shard_map/all_gather | solution.py:13
  168.0 1.6 copy-start.1
  168.0 2.5 copy-start.4
  168.0 2.9 copy-start.2
  168.0 95.4 %copy-start.3 = (f32[1,128,128]{2,1,0:T(8,128)S(1)}, f32[1,128,128]{2,1,0:T(8,128)}, u32[]{:S(2)}) copy-start(f32[1,128,128]{2,1,0:T(8,128)} %param.13) | copy-start | bytes 196612
  170.4 159.9 %all-gather.7.cloned.1.call-start = ((), (), s32[]{:S(2)}) async-start(), calls=%async_computation.4 | async-start | bytes 1081344 | tf_op jit(solution)/shard_map/all_gather | solution.py:13
  264.7 223.8 %reduce-scatter.4.cloned.1.call-start = ((), (), s32[]{:S(2)}) async-start(), calls=%async_computation.5 | async-start | bytes 3244032
  364.3 301.1 %all-reduce.2.cloned.1.call-start = ((), (), s32[]{:S(2)}) async-start(), calls=%async_computation.2 | async-start | bytes 4194304 | tf_op jit(solution)/shard_map/psum | solution.py:103
Sparse Core Ops, SparseCore 0:
  170.5 67.0 all-gather.4
  264.8 65.4 all-gather.6
  364.4 124.0 reduce-scatter.3
  492.1 173.2 all-reduce.1
